TPU v7x, 32 devices: a whole 2x2x4 slice. The times are simulated.
32 devices in a mesh: dp: 8 (over z, y), tensor: 4 (over x, core).
Axes of the slice: x: 2, y: 2, z: 4, core: 2. Of those that a mesh axis runs over, the one named last changes fastest.
Arguments:
- tokens: bfloat16 [18464, 1024], P(('dp', 'tensor')), may hold values from -6 to 6
- cotangent: bfloat16 [18464, 1024], P(('dp', 'tensor')), may hold values from -6 to 6
- image_mask: int32 [32], P('dp'), may hold values 0 or 1
- query_weight: float32 [1024, 1024], P('dp', 'tensor'), may hold values from -0.1875 to 0.1875
- key_weight: float32 [1024, 1024], P('dp', 'tensor'), may hold values from -0.1875 to 0.1875
- value_weight: float32 [1024, 1024], P('dp', 'tensor'), may hold values from -0.1875 to 0.1875
- out_weight: float32 [1024, 1024], P('tensor', 'dp'), may hold values from -1 to 1
- up_weight: float32 [1024, 4096], P('dp', 'tensor'), may hold values from -0.1875 to 0.1875
- down_weight: float32 [4096, 1024], P('tensor', 'dp'), may hold values from -0.1875 to 0.1875
- query_bias: float32 [16, 64], P('tensor', 'dp'), may hold values from -3 to 3
- value_bias: float32 [16, 64], P('tensor', 'dp'), may hold values from -3 to 3
- up_bias: float32 [32, 128], P('tensor', 'dp'), may hold values from -3 to 3
- attn_gain: float32 [1024], P('dp'), may hold values from 0.1 to 1.9
- attn_shift: float32 [1024], P('dp'), may hold values from -3 to 3
- mlp_gain: float32 [1024], P('dp'), may hold values from 0.1 to 1.9
- mlp_shift: float32 [1024], P('dp'), may hold values from -3 to 3
- out_bias: float32 [1024], P('dp'), may hold values from -3 to 3
- down_bias: float32 [1024], P('dp'), may hold values from -3 to 3
Outputs:
- block_out: bfloat16 [18464, 1024], P(('dp', 'tensor'))
- tokens_grad: float32 [18464, 1024], P(('dp', 'tensor'))
- query_weight_grad: float32 [1024, 1024], P('dp', 'tensor')
- key_weight_grad: float32 [1024, 1024], P('dp', 'tensor')
- value_weight_grad: float32 [1024, 1024], P('dp', 'tensor')
- out_weight_grad: float32 [1024, 1024], P('tensor', 'dp')
- up_weight_grad: float32 [1024, 4096], P('dp', 'tensor')
- down_weight_grad: float32 [4096, 1024], P('tensor', 'dp')
- query_bias_grad: float32 [16, 64], P('tensor', 'dp')
- value_bias_grad: float32 [16, 64], P('tensor', 'dp')
- up_bias_grad: float32 [32, 128], P('tensor', 'dp')
- attn_gain_grad: float32 [1024], P('dp')
- attn_shift_grad: float32 [1024], P('dp')
- mlp_gain_grad: float32 [1024], P('dp')
- mlp_shift_grad: float32 [1024], P('dp')
- out_bias_grad: float32 [1024], P('dp')
- down_bias_grad: float32 [1024], P('dp')
All inputs are finite; a program needn't handle non-finite values. No bound on the sum of `image_mask` on one device may be relied on, other than what follows from the above.
Results may differ from a plain program's by a relative error of at most 0.018.
Values may be sent and summed in bfloat16 or wider, within the bound.
A program may use at most 192 MiB of HBM per device.

v0:
```python
import math

import jax
import jax.numpy as jnp
from jax import lax
from jax.sharding import PartitionSpec as P

HD = 64
SEQ = 577


EPS = 1e-05
SLOPE = 1.702


def normalize(values, gain, shift):
    centre = values - jnp.mean(values, axis=-1, keepdims=True)
    inverse = lax.rsqrt(jnp.mean(centre * centre, axis=-1, keepdims=True) + EPS)
    normed = centre * inverse
    return (normed * gain + shift, normed, inverse)


def normalize_back(grad_out, normed, inverse, gain):
    scaled = grad_out * gain
    grad_in = inverse * (
        scaled
        - jnp.mean(scaled, axis=-1, keepdims=True)
        - normed * jnp.mean(scaled * normed, axis=-1, keepdims=True)
    )
    return (grad_in, jnp.sum(grad_out * normed, axis=0), jnp.sum(grad_out, axis=0))


def attend_image(pieces):
    query, key, value = pieces
    scale = 1.0 / math.sqrt(query.shape[-1])
    scores = jnp.einsum("qhd,khd->hqk", query, key, preferred_element_type=jnp.float32) * scale
    highest = jnp.max(scores, axis=-1, keepdims=True)
    expo = jnp.exp(scores - highest)
    total = jnp.sum(expo, axis=-1, keepdims=True)
    probs = (expo / total).astype(jnp.bfloat16)
    mixed = jnp.einsum("hqk,khd->qhd", probs, value, preferred_element_type=jnp.float32)
    return (mixed.astype(jnp.bfloat16), (highest + jnp.log(total))[..., 0])


def attend_back(pieces):
    query, key, value, grad_mixed, log_total = pieces
    scale = 1.0 / math.sqrt(query.shape[-1])
    scores = jnp.einsum("qhd,khd->hqk", query, key, preferred_element_type=jnp.float32) * scale
    probs = jnp.exp(scores - log_total[..., None])
    grad_value = jnp.einsum(
        "hqk,qhd->khd", probs.astype(jnp.bfloat16), grad_mixed, preferred_element_type=jnp.float32
    ).astype(jnp.bfloat16)
    grad_probs = jnp.einsum("qhd,khd->hqk", grad_mixed, value, preferred_element_type=jnp.float32)
    grad_scores = probs * (grad_probs - jnp.sum(grad_probs * probs, axis=-1, keepdims=True))
    grad_scores = grad_scores.astype(jnp.bfloat16)
    grad_query = (
        jnp.einsum("hqk,khd->qhd", grad_scores, key, preferred_element_type=jnp.float32) * scale
    )
    grad_key = (
        jnp.einsum("hqk,qhd->khd", grad_scores, query, preferred_element_type=jnp.float32) * scale
    )
    return (grad_query.astype(jnp.bfloat16), grad_key.astype(jnp.bfloat16), grad_value)


def on_device(
    tokens,
    cotangent,
    image_mask,
    query_weight,
    key_weight,
    value_weight,
    out_weight,
    up_weight,
    down_weight,
    query_bias,
    value_bias,
    up_bias,
    attn_gain,
    attn_shift,
    mlp_gain,
    mlp_shift,
    out_bias,
    down_bias,
):
    rows = tokens.shape[0]
    gathered = (
        lax.all_gather(query_weight.astype(jnp.bfloat16), "dp", axis=0, tiled=True),
        lax.all_gather(key_weight.astype(jnp.bfloat16), "dp", axis=0, tiled=True),
        lax.all_gather(value_weight.astype(jnp.bfloat16), "dp", axis=0, tiled=True),
        lax.all_gather(out_weight.astype(jnp.bfloat16), "dp", axis=1, tiled=True),
        lax.all_gather(up_weight.astype(jnp.bfloat16), "dp", axis=0, tiled=True),
        lax.all_gather(down_weight.astype(jnp.bfloat16), "dp", axis=1, tiled=True),
        lax.all_gather(query_bias.astype(jnp.bfloat16), "dp", axis=1, tiled=True),
        lax.all_gather(value_bias.astype(jnp.bfloat16), "dp", axis=1, tiled=True),
        lax.all_gather(up_bias.astype(jnp.bfloat16), "dp", axis=1, tiled=True),
        lax.all_gather(attn_gain.astype(jnp.bfloat16), "dp", axis=0, tiled=True),
        lax.all_gather(attn_shift.astype(jnp.bfloat16), "dp", axis=0, tiled=True),
        lax.all_gather(mlp_gain.astype(jnp.bfloat16), "dp", axis=0, tiled=True),
        lax.all_gather(mlp_shift.astype(jnp.bfloat16), "dp", axis=0, tiled=True),
        lax.all_gather(out_bias.astype(jnp.bfloat16), "dp", axis=0, tiled=True),
        lax.all_gather(down_bias.astype(jnp.bfloat16), "dp", axis=0, tiled=True),
    )
    (
        full_query,
        full_key,
        full_value,
        full_out,
        full_up,
        full_down,
        gbias_query,
        gbias_value,
        gbias_up,
        gain_attn,
        shift_attn,
        gain_mlp,
        shift_mlp,
        gbias_out,
        gbias_down,
    ) = gathered
    vec_query = gbias_query.astype(jnp.float32).reshape(-1)
    vec_value = gbias_value.astype(jnp.float32).reshape(-1)
    gain_a = gain_attn.astype(jnp.float32)
    shift_a = shift_attn.astype(jnp.float32)
    gain_m = gain_mlp.astype(jnp.float32)
    shift_m = shift_mlp.astype(jnp.float32)
    vec_out = gbias_out.astype(jnp.float32)
    vec_down = gbias_down.astype(jnp.float32)
    local_width = full_query.shape[1]
    heads_here = local_width // HD
    position = lax.axis_index("tensor") * rows + jnp.arange(rows, dtype=jnp.int32)
    slot_index = position // SEQ
    slot_range = jnp.arange(image_mask.shape[0], dtype=jnp.int32)
    row_mask = jnp.sum(
        jnp.where(slot_index[:, None] == slot_range[None, :], image_mask[None, :], 0), axis=1
    ).astype(jnp.float32)[:, None]
    inputs = tokens.astype(jnp.float32)
    normed_a, unit_a, inverse_a = normalize(inputs, gain_a, shift_a)
    attn_in = lax.all_gather(normed_a.astype(jnp.bfloat16), "tensor", axis=0, tiled=True)
    group_rows = attn_in.shape[0]
    images = group_rows // SEQ
    query = (jnp.dot(attn_in, full_query, preferred_element_type=jnp.float32) + vec_query).astype(
        jnp.bfloat16
    )
    key = jnp.dot(attn_in, full_key, preferred_element_type=jnp.float32).astype(jnp.bfloat16)
    value = (jnp.dot(attn_in, full_value, preferred_element_type=jnp.float32) + vec_value).astype(
        jnp.bfloat16
    )
    shaped = (images, SEQ, heads_here, HD)
    query_img = query.reshape(shaped)
    key_img = key.reshape(shaped)
    value_img = value.reshape(shaped)
    mixed_img, log_total = lax.map(attend_image, (query_img, key_img, value_img))
    mixed = mixed_img.reshape(group_rows, local_width)
    middle = (
        inputs
        + lax.psum_scatter(
            jnp.dot(mixed, full_out, preferred_element_type=jnp.float32).astype(jnp.bfloat16),
            "tensor",
            scatter_dimension=0,
            tiled=True,
        ).astype(jnp.float32)
        + vec_out
    )
    normed_m, unit_m, inverse_m = normalize(middle, gain_m, shift_m)
    grad_out = cotangent.astype(jnp.float32) * row_mask
    grad_down_b = jnp.sum(grad_out, axis=0)
    whole_up, whole_down, whole_up_b = (
        lax.all_gather(full_up, "tensor", axis=1, tiled=True),
        lax.all_gather(full_down, "tensor", axis=0, tiled=True),
        lax.all_gather(gbias_up, "tensor", axis=0, tiled=True),
    )
    vec_up = whole_up_b.astype(jnp.float32).reshape(-1)
    mlp_in = normed_m.astype(jnp.bfloat16)
    pre = jnp.dot(mlp_in, whole_up, preferred_element_type=jnp.float32) + vec_up
    sigma = jax.nn.sigmoid(SLOPE * pre)
    hidden = (pre * sigma).astype(jnp.bfloat16)
    branch = jnp.dot(hidden, whole_down, preferred_element_type=jnp.float32)
    block_out = ((middle + branch + vec_down) * row_mask).astype(jnp.bfloat16)
    grad_branch = grad_out.astype(jnp.bfloat16)
    whole_down_grad = jnp.einsum(
        "rf,rd->fd", hidden, grad_branch, preferred_element_type=jnp.float32
    )
    grad_hidden = jnp.einsum(
        "rd,fd->rf", grad_branch, whole_down, preferred_element_type=jnp.float32
    )
    grad_pre = (grad_hidden * (sigma + SLOPE * pre * sigma * (1.0 - sigma))).astype(jnp.bfloat16)
    whole_up_b_grad = jnp.sum(grad_pre.astype(jnp.float32), axis=0)
    whole_up_grad = jnp.einsum("rd,rf->df", mlp_in, grad_pre, preferred_element_type=jnp.float32)
    grad_normed_m = jnp.einsum("rf,df->rd", grad_pre, whole_up, preferred_element_type=jnp.float32)
    grad_up_w, grad_down_w, grad_up_rows = (
        lax.psum_scatter(
            whole_up_grad.astype(jnp.bfloat16), "tensor", scatter_dimension=1, tiled=True
        ).astype(jnp.float32),
        lax.psum_scatter(
            whole_down_grad.astype(jnp.bfloat16), "tensor", scatter_dimension=0, tiled=True
        ).astype(jnp.float32),
        lax.psum_scatter(
            whole_up_b_grad.reshape(-1, 128).astype(jnp.bfloat16),
            "tensor",
            scatter_dimension=0,
            tiled=True,
        ).astype(jnp.float32),
    )
    grad_up_b = grad_up_rows.reshape(-1)
    grad_mid_norm, grad_gain_m, grad_shift_m = normalize_back(
        grad_normed_m, unit_m, inverse_m, gain_m
    )
    grad_middle = grad_out + grad_mid_norm
    grad_out_b = jnp.sum(grad_middle, axis=0)
    grad_attn = lax.all_gather(grad_middle.astype(jnp.bfloat16), "tensor", axis=0, tiled=True)
    grad_out_w = jnp.einsum("rh,rd->hd", mixed, grad_attn, preferred_element_type=jnp.float32)
    grad_mixed = jnp.einsum(
        "rd,hd->rh", grad_attn, full_out, preferred_element_type=jnp.float32
    ).astype(jnp.bfloat16)
    grad_q_img, grad_k_img, grad_v_img = lax.map(
        attend_back, (query_img, key_img, value_img, grad_mixed.reshape(shaped), log_total)
    )
    grad_query = grad_q_img.reshape(group_rows, local_width)
    grad_key = grad_k_img.reshape(group_rows, local_width)
    grad_value = grad_v_img.reshape(group_rows, local_width)
    grad_query_w = jnp.einsum("rd,rh->dh", attn_in, grad_query, preferred_element_type=jnp.float32)
    grad_key_w = jnp.einsum("rd,rh->dh", attn_in, grad_key, preferred_element_type=jnp.float32)
    grad_value_w = jnp.einsum("rd,rh->dh", attn_in, grad_value, preferred_element_type=jnp.float32)
    grad_query_b = jnp.sum(grad_query.astype(jnp.float32), axis=0).reshape(heads_here, HD)
    grad_value_b = jnp.sum(grad_value.astype(jnp.float32), axis=0).reshape(heads_here, HD)
    total = jnp.einsum("rh,dh->rd", grad_query, full_query, preferred_element_type=jnp.float32)
    total = total + jnp.einsum("rh,dh->rd", grad_key, full_key, preferred_element_type=jnp.float32)
    grad_normed_a = lax.psum_scatter(
        (
            total
            + jnp.einsum("rh,dh->rd", grad_value, full_value, preferred_element_type=jnp.float32)
        ).astype(jnp.bfloat16),
        "tensor",
        scatter_dimension=0,
        tiled=True,
    ).astype(jnp.float32)
    grad_in_norm, grad_gain_a, grad_shift_a = normalize_back(
        grad_normed_a, unit_a, inverse_a, gain_a
    )
    tokens_grad = grad_middle + grad_in_norm
    vectors = lax.psum(
        (grad_gain_a, grad_shift_a, grad_gain_m, grad_shift_m, grad_out_b, grad_down_b), "tensor"
    )
    sent = (
        lax.psum_scatter(grad_query_w, "dp", scatter_dimension=0, tiled=True),
        lax.psum_scatter(grad_key_w, "dp", scatter_dimension=0, tiled=True),
        lax.psum_scatter(grad_value_w, "dp", scatter_dimension=0, tiled=True),
        lax.psum_scatter(grad_out_w, "dp", scatter_dimension=1, tiled=True),
        lax.psum_scatter(grad_up_w, "dp", scatter_dimension=0, tiled=True),
        lax.psum_scatter(grad_down_w, "dp", scatter_dimension=1, tiled=True),
        lax.psum_scatter(grad_query_b, "dp", scatter_dimension=1, tiled=True),
        lax.psum_scatter(grad_value_b, "dp", scatter_dimension=1, tiled=True),
        lax.psum_scatter(grad_up_b.reshape(-1, 128), "dp", scatter_dimension=1, tiled=True),
        lax.psum_scatter(vectors[0], "dp", scatter_dimension=0, tiled=True),
        lax.psum_scatter(vectors[1], "dp", scatter_dimension=0, tiled=True),
        lax.psum_scatter(vectors[2], "dp", scatter_dimension=0, tiled=True),
        lax.psum_scatter(vectors[3], "dp", scatter_dimension=0, tiled=True),
        lax.psum_scatter(vectors[4], "dp", scatter_dimension=0, tiled=True),
        lax.psum_scatter(vectors[5], "dp", scatter_dimension=0, tiled=True),
    )
    return (
        block_out,
        tokens_grad,
        sent[0],
        sent[1],
        sent[2],
        sent[3],
        sent[4],
        sent[5],
        sent[6],
        sent[7],
        sent[8],
        sent[9],
        sent[10],
        sent[11],
        sent[12],
        sent[13],
        sent[14],
    )


def solution(mesh):
    in_specs = (
        P(("dp", "tensor"), None),
        P(("dp", "tensor"), None),
        P("dp"),
        P("dp", "tensor"),
        P("dp", "tensor"),
        P("dp", "tensor"),
        P("tensor", "dp"),
        P("dp", "tensor"),
        P("tensor", "dp"),
        P("tensor", "dp"),
        P("tensor", "dp"),
        P("tensor", "dp"),
        P("dp"),
        P("dp"),
        P("dp"),
        P("dp"),
        P("dp"),
        P("dp"),
    )
    out_specs = (
        P(("dp", "tensor"), None),
        P(("dp", "tensor"), None),
        P("dp", "tensor"),
        P("dp", "tensor"),
        P("dp", "tensor"),
        P("tensor", "dp"),
        P("dp", "tensor"),
        P("tensor", "dp"),
        P("tensor", "dp"),
        P("tensor", "dp"),
        P("tensor", "dp"),
        P("dp"),
        P("dp"),
        P("dp"),
        P("dp"),
        P("dp"),
        P("dp"),
    )
    return jax.shard_map(
        on_device, mesh=mesh, in_specs=in_specs, out_specs=out_specs, check_vma=False
    )
```

profile of v0, /device:TPU:0, one launch (start us, length us, event | category | flops | bytes accessed | tf_op | source)
XLA Modules:
  0.0 1200.4 jit_solution(13877576292232570344)
XLA Ops:
  11.7 22.2 %all-gather.1 = bf16[8,1,128]{2,1,0:T(2,128)(2,1)S(1)} all-gather(bf16[1,1,128]{2,1,0:T(2,128)(2,1)S(1)} %convert_bitcast_fusion.8), channel_id=1, replica_groups=mesh['dp'=8,'tensor'=4] {'dp'}, dimensions={0}, use_global_device_ids=true | all-gather | bytes 2304 | tf_op jit(solution)/shard_map/all_gather | solution.py:97
  34.5 16.3 %all-gather = bf16[8,1,128]{2,1,0:T(2,128)(2,1)S(1)} all-gather(bf16[1,1,128]{2,1,0:T(2,128)(2,1)S(1)} %convert_bitcast_fusion.9), channel_id=1, replica_groups=mesh['dp'=8,'tensor'=4] {'dp'}, dimensions={0}, use_global_device_ids=true | all-gather | bytes 2304 | tf_op jit(solution)/shard_map/all_gather | solution.py:96
  53.8 9.2 all-gather.18.cloned.1.call-done
  63.1 18.2 %all-gather.4 = bf16[8,8,4]{1,2,0:T(4,128)(2,1)S(1)} all-gather(bf16[1,8,4]{1,2,0:T(4,128)(2,1)S(1)} %convert_bitcast_fusion.2), channel_id=1, replica_groups=mesh['dp'=8,'tensor'=4] {'dp'}, dimensions={0}, use_global_device_ids=true | all-gather | bytes 576 | tf_op jit(solution)/shard_map/all_gather | solution.py:93
  81.4 16.4 %all-gather.3 = bf16[8,8,4]{1,2,0:T(4,128)(2,1)S(1)} all-gather(bf16[1,8,4]{1,2,0:T(4,128)(2,1)S(1)} %convert_bitcast_fusion.3), channel_id=1, replica_groups=mesh['dp'=8,'tensor'=4] {'dp'}, dimensions={0}, use_global_device_ids=true | all-gather | bytes 576 | tf_op jit(solution)/shard_map/all_gather | solution.py:94
  98.6 26.1 %all-gather.8 = bf16[8,16,8]{1,2,0:T(8,128)(2,1)S(1)} all-gather(bf16[1,16,8]{1,2,0:T(8,128)(2,1)S(1)} %convert_bitcast_fusion.1), channel_id=1, replica_groups=mesh['dp'=8,'tensor'=4] {'dp'}, dimensions={0}, use_global_device_ids=true | all-gather | bytes 2304 | tf_op jit(solution)/shard_map/all_gather | solution.py:95
  132.9 28.7 %all_gather.68 = bf16[256,1024]{1,0:T(8,128)(2,1)} all-gather(bf16[256,128]{1,0:T(8,128)(2,1)S(1)} %convert_element_type.199), channel_id=1, replica_groups=mesh['dp'=8,'tensor'=4] {'dp'}, dimensions={1}, use_global_device_ids=true | all-gather | bytes 589824 | tf_op jit(solution)/shard_map/all_gather | solution.py:90
  161.5 31.3 %all_gather.63 = bf16[1024,256]{1,0:T(8,128)(2,1)S(1)} all-gather(bf16[128,256]{1,0:T(8,128)(2,1)S(1)} %convert_element_type.191), channel_id=1, replica_groups=mesh['dp'=8,'tensor'=4] {'dp'}, dimensions={0}, use_global_device_ids=true | all-gather | bytes 589824 | tf_op jit(solution)/shard_map/all_gather | solution.py:89
  192.8 31.4 %all_gather.67 = bf16[1024,256]{1,0:T(8,128)(2,1)S(1)} all-gather(bf16[128,256]{1,0:T(8,128)(2,1)S(1)} %convert_element_type.197), channel_id=1, replica_groups=mesh['dp'=8,'tensor'=4] {'dp'}, dimensions={0}, use_global_device_ids=true | all-gather | bytes 589824 | tf_op jit(solution)/shard_map/all_gather | solution.py:88
  224.3 31.2 %all_gather.65 = bf16[1024,256]{1,0:T(8,128)(2,1)S(1)} all-gather(bf16[128,256]{1,0:T(8,128)(2,1)S(1)} %convert_element_type.194), channel_id=1, replica_groups=mesh['dp'=8,'tensor'=4] {'dp'}, dimensions={0}, use_global_device_ids=true | all-gather | bytes 589824 | tf_op jit(solution)/shard_map/all_gather | solution.py:87
  303.7 25.3 %while.26 = (s32[]{:T(128)}, bf16[4,577,4,64]{1,3,2,0:T(8,128)(2,1)}, f32[4,4,577]{2,1,0:T(4,128)S(1)}, bf16[4,577,4,64]{1,3,2,0:T(8,128)(2,1)}, bf16[4,577,4,64...) while((s32[]{:T(128)}, bf16[4,577,4,64]{1,3,2,0:T(8,128)(2,1)}, ...), condition=%wide.region_5.6_spmd, body=%wide.region_2.5_spmd.sunk | while | flops 353050112 | bytes 17370328 | solution.py:152
  341.0 45.7 %fusion = bf16[584,1024]{1,0:T(8,128)(2,1)} fusion(bf16[2308,1024]{1,0:T(8,128)(2,1)} %convolution_convert_fusion.2), kind=kCustom, calls=%all-reduce-scatter | all-reduce-scatter fusion | flops 2392065 | bytes 5923328
  388.9 16.3 %all-gather.5 = bf16[8,1,128]{2,1,0:T(2,128)(2,1)S(1)} all-gather(bf16[1,1,128]{2,1,0:T(2,128)(2,1)S(1)} %copy-done.43), channel_id=1, replica_groups=mesh['dp'=8,'tensor'=4] {'dp'}, dimensions={0}, use_global_device_ids=true | all-gather | bytes 2304 | tf_op jit(solution)/shard_map/all_gather | solution.py:100
  405.2 18.0 %all-gather.7 = bf16[8,1,128]{2,1,0:T(2,128)(2,1)S(1)} all-gather(bf16[1,1,128]{2,1,0:T(2,128)(2,1)S(1)} %copy-done.42), channel_id=1, replica_groups=mesh['dp'=8,'tensor'=4] {'dp'}, dimensions={0}, use_global_device_ids=true | all-gather | bytes 2304 | tf_op jit(solution)/shard_map/all_gather | solution.py:99
  423.3 16.3 %all-gather.6 = bf16[8,1,128]{2,1,0:T(2,128)(2,1)S(1)} all-gather(bf16[1,1,128]{2,1,0:T(2,128)(2,1)S(1)} %copy-done.41), channel_id=1, replica_groups=mesh['dp'=8,'tensor'=4] {'dp'}, dimensions={0}, use_global_device_ids=true | all-gather | bytes 2304 | tf_op jit(solution)/shard_map/all_gather | solution.py:98
  451.1 11.6 fusion.84
  462.7 13.8 %fusion.87 = (bf16[4096]{0:T(1024)(128)(2,1)S(1)}, bf16[577,4096]{1,0:T(8,128)(2,1)}) fusion(f32[577,4096]{1,0:T(8,128)} %fusion.84, f32[4096]{0:T(1024)S(1)} %copy-done.32, bf16[4096,1024]{1,0:T(8,128)(2,1)} %all-gather.24.cloned.1.call-done, bf16[577,1024]{1,0:T(8,128)(2,1)} %param.23, f32[577]{0:T(1024)S(1)} %convert_element_type.215), kind=kOutput, calls=%fused_computation.144 | convolution fusion | flops 4870355968 | bytes 23777540 | tf_op jit(solution)/shard_map/rd,fd->rf/dot_general | solution.py:183
  476.6 9.4 multiply_reduce_fusion.2
  491.2 12.3 %convolution_convert_fusion.1 = bf16[4096,1024]{1,0:T(8,128)(2,1)} fusion(bf16[577,1024]{1,0:T(8,128)(2,1)} %param.23, f32[577]{0:T(1024)S(1)} %convert_element_type.215, f32[577,4096]{1,0:T(8,128)} %fusion.84, f32[4096]{0:T(1024)S(1)} %copy-done.32), kind=kOutput, calls=%fused_computation.65 | convolution fusion | flops 4862737408 | bytes 19042564 | tf_op jit(solution)/shard_map/rf,rd->fd/dot_general | solution.py:180
  511.5 12.7 %convolution_convert_fusion = bf16[1024,4096]{1,0:T(8,128)(2,1)} fusion(bf16[577,4096]{1,0:T(8,128)(2,1)} %get-tuple-element.242, f32[1024]{0:T(1024)S(1)} %bitcast.220, f32[1024]{0:T(1024)S(1)} %bitcast.212, f32[577]{0:T(1024)S(1)} %add_rsqrt_fusion, f32[577]{0:T(1024)S(1)} %broadcast_multiply_fusion.4, f32[1024]{0:T(1024)S(1)} %bitcast.204, ...), kind=kOutput, calls=%fused_computation.64 | convolution fusion | flops 4849738752 | bytes 15567372 | tf_op jit(solution)/shard_map/rd,rf->df/dot_general | solution.py:188
  557.6 48.6 %while.27 = (s32[]{:T(128)}, bf16[4,577,4,64]{1,3,2,0:T(8,128)(2,1)}, bf16[4,577,4,64]{1,3,2,0:T(8,128)(2,1)}, bf16[4,577,4,64]{1,3,2,0:T(8,128)(2,1)}, bf16[4,5...) while((s32[]{:T(128)}, ...), condition=%wide.region_14.15_spmd, body=%wide.region_12.14_spmd.sunk | while | flops 869015040 | bytes 49660204 | solution.py:215
  646.0 20.6 %all-gather.9 = bf16[8,1,128]{2,1,0:T(2,128)(2,1)S(1)} all-gather(bf16[1,1,128]{2,1,0:T(2,128)(2,1)S(1)} %convert_bitcast_fusion.4), channel_id=1, replica_groups=mesh['dp'=8,'tensor'=4] {'dp'}, dimensions={0}, use_global_device_ids=true | all-gather | bytes 2304 | tf_op jit(solution)/shard_map/all_gather | solution.py:101
  666.7 12.8 %multiply_convert_fusion.3 = bf16[577,1024]{1,0:T(8,128)(2,1)} fusion(bf16[4096,1024]{1,0:T(8,128)(2,1)} %all-gather.24.cloned.1.call-done, f32[577]{0:T(1024)S(1)} %convert_element_type.215, f32[1024]{0:T(1024)S(1)} %bitcast.221, f32[1024]{0:T(1024)S(1)} %bitcast.205, bf16[605,1024]{1,0:T(8,128)(2,1)S(1)} %copy-done.4, u32[]{:S(6)} %subtract, ...), kind=kOutput, calls=%fused_computation.103 | convolution fusion | flops 4861497344 | bytes 21414152 | tf_op jit(solution)/shard_map/dot_general | solution.py:177
  680.9 61.3 %reduce-scatter.26.cloned.1.call-done = bf16[1024,1024]{1,0:T(8,128)(2,1)} async-done(((bf16[1024,4096]{1,0:T(8,128)(2,1)}), bf16[1024,1024]{1,0:T(8,128)(2,1)}) %reduce-scatter.26.cloned.1.call-update) | async-done | bytes 2097168 | tf_op jit(solution)/shard_map/reduce_scatter | solution.py:191
  755.8 45.6 %fusion.1 = bf16[584,1024]{1,0:T(8,128)(2,1)} fusion(bf16[2308,1024]{1,0:T(8,128)(2,1)} %add_convert_fusion), kind=kCustom, calls=%all-reduce-scatter.1 | all-reduce-scatter fusion | flops 2392065 | bytes 5923328
  812.6 37.1 %all-reduce.13 = (f32[4,64]{1,0:T(4,128)S(1)}, f32[4,64]{1,0:T(4,128)S(1)}, f32[1024]{0:T(1024)S(1)}, f32[1024]{0:T(1024)S(1)}, f32[1024]{0:T(1024)S(1)}, /*inde...) all-reduce(f32[4,64]{1,0:T(4,128)S(1)} %convert_reduce_fusion.3, ...), channel_id=12, replica_groups=mesh['dp'=8,'tensor'=4] {'dp'}, use_global_device_ids=true, to_apply=%region_27.28.clone | all-reduce | flops 6656 | bytes 53248
  850.1 7.5 all-reduce.14
  863.1 13.7 %reduce-scatter.18.cloned.1.call-done = f32[128,256]{1,0:T(8,128)} async-done(((f32[1024,256]{1,0:T(8,128)}), f32[128,256]{1,0:T(8,128)}) %reduce-scatter.18.cloned.1.call-update) | async-done | bytes 131088 | tf_op jit(solution)/shard_map/reduce_scatter | solution.py:245
  876.7 66.2 %reduce-scatter.20.cloned.1.call-done = f32[128,256]{1,0:T(8,128)} async-done(((f32[1024,256]{1,0:T(8,128)}), f32[128,256]{1,0:T(8,128)}) %reduce-scatter.20.cloned.1.call-update) | async-done | bytes 131088 | tf_op jit(solution)/shard_map/reduce_scatter | solution.py:246
  943.0 66.9 %reduce-scatter.22.cloned.1.call-done = f32[128,256]{1,0:T(8,128)} async-done(((f32[1024,256]{1,0:T(8,128)}), f32[128,256]{1,0:T(8,128)}) %reduce-scatter.22.cloned.1.call-update) | async-done | bytes 131088 | tf_op jit(solution)/shard_map/reduce_scatter | solution.py:247
  1009.9 91.4 %reduce-scatter.32.cloned.1.call-done = f32[1024,128]{1,0:T(8,128)} async-done(((f32[1024,1024]{1,0:T(8,128)}), f32[1024,128]{1,0:T(8,128)}) %reduce-scatter.32.cloned.1.call-update) | async-done | bytes 524304 | tf_op jit(solution)/shard_map/reduce_scatter | solution.py:250
  1101.2 92.2 %reduce-scatter.28.cloned.1.call-done = f32[128,1024]{1,0:T(8,128)} async-done(((f32[1024,1024]{1,0:T(8,128)}), f32[128,1024]{1,0:T(8,128)}) %reduce-scatter.28.cloned.1.call-update) | async-done | bytes 524304 | tf_op jit(solution)/shard_map/reduce_scatter | solution.py:249
  (299 shorter events, 280.0 us)
Async XLA Ops:
  7.2 55.7 %all-gather.18.cloned.1.call-start = ((), (), s32[]{:S(2)}) async-start(), calls=%async_computation.9 | async-start | bytes 2359296 | tf_op jit(solution)/shard_map/all_gather | solution.py:91
  9.1 246.3 %all-gather.22.cloned.1.call-start = ((), (), s32[]{:S(2)}) async-start(), calls=%async_computation.11 | async-start | bytes 2359296 | tf_op jit(solution)/shard_map/all_gather | solution.py:92
  11.0 244.6 %all-gather.26.cloned.1.call-start = ((), (), s32[]{:S(2)}) async-start(), calls=%async_computation.21 | async-start | bytes 5980160 | tf_op jit(solution)/shard_map/all_gather | solution.py:138
  52.1 72.7 %copy-start.19 = (f32[128,256]{1,0:T(8,128)S(1)}, f32[128,256]{1,0:T(8,128)}, u32[]{:S(2)}) copy-start(f32[128,256]{1,0:T(8,128)} %param.25) | copy-start | bytes 393220
  53.7 71.2 %copy-start.20 = (f32[128,256]{1,0:T(8,128)S(1)}, f32[128,256]{1,0:T(8,128)}, u32[]{:S(2)}) copy-start(f32[128,256]{1,0:T(8,128)} %param.26) | copy-start | bytes 393220
  53.7 71.2 %copy-start.21 = (f32[128,256]{1,0:T(8,128)S(1)}, f32[128,256]{1,0:T(8,128)}, u32[]{:S(2)}) copy-start(f32[128,256]{1,0:T(8,128)} %param.27) | copy-start | bytes 393220
  53.7 71.2 %copy-start.22 = (f32[256,128]{1,0:T(8,128)S(1)}, f32[256,128]{1,0:T(8,128)}, u32[]{:S(2)}) copy-start(f32[256,128]{1,0:T(8,128)} %param.28) | copy-start | bytes 393220
  53.7 77.0 %copy-start.45 = (f32[128]{0:T(128)S(1)}, f32[128]{0:T(128)}, u32[]{:S(2)}) copy-start(f32[128]{0:T(128)} %param.36) | copy-start | bytes 1540
  53.7 77.6 %copy-start.46 = (f32[128]{0:T(128)S(1)}, f32[128]{0:T(128)}, u32[]{:S(2)}) copy-start(f32[128]{0:T(128)} %param.37) | copy-start | bytes 1540
  53.7 78.1 %copy-start.47 = (f32[128]{0:T(128)S(1)}, f32[128]{0:T(128)}, u32[]{:S(2)}) copy-start(f32[128]{0:T(128)} %param.38) | copy-start | bytes 1540
  53.7 397.4 %all-gather.20.cloned.1.call-start = ((), (), s32[]{:S(2)}) async-start(), calls=%async_computation.10 | async-start | bytes 10485760 | tf_op jit(solution)/shard_map/all_gather | solution.py:168
  63.0 399.7 %all-gather.24.cloned.1.call-start = ((), (), s32[]{:S(2)}) async-start(), calls=%async_computation.12 | async-start | bytes 10485760 | tf_op jit(solution)/shard_map/all_gather | solution.py:169
  192.8 82.5 %copy-start.11 = (bf16[1024,256]{1,0:T(8,128)(2,1)}, bf16[1024,256]{1,0:T(8,128)(2,1)S(1)}, u32[]{:S(2)}) copy-start(bf16[1024,256]{1,0:T(8,128)(2,1)S(1)} %all_gather.63) | copy-start | bytes 1572868
  224.3 64.6 %copy-start.15 = (bf16[1024,256]{1,0:T(8,128)(2,1)}, bf16[1024,256]{1,0:T(8,128)(2,1)S(1)}, u32[]{:S(2)}) copy-start(bf16[1024,256]{1,0:T(8,128)(2,1)S(1)} %all_gather.67) | copy-start | bytes 1572868
  255.5 273.3 %all-gather.28.cloned.1.call-start = ((), (), s32[]{:S(2)}) async-start(), calls=%async_computation.22 | async-start | bytes 5980160 | tf_op jit(solution)/shard_map/all_gather | solution.py:210
  341.0 47.8 %copy-start.40 = (s32[4]{0:T(128)S(1)}, s32[4]{0:T(128)}, u32[]{:S(2)}) copy-start(s32[4]{0:T(128)} %param.24) | copy-start | bytes 52
  341.0 47.9 %copy-start.43 = (bf16[1,1,128]{2,1,0:T(2,128)(2,1)S(1)}, bf16[1,1,128]{2,1,0:T(2,128)(2,1)}, u32[]{:S(2)}) copy-start(bf16[1,1,128]{2,1,0:T(2,128)(2,1)} %convert_bitcast_fusion.7) | copy-start | bytes 772
  341.0 64.3 %copy-start.42 = (bf16[1,1,128]{2,1,0:T(2,128)(2,1)S(1)}, bf16[1,1,128]{2,1,0:T(2,128)(2,1)}, u32[]{:S(2)}) copy-start(bf16[1,1,128]{2,1,0:T(2,128)(2,1)} %convert_bitcast_fusion.5) | copy-start | bytes 772
  341.0 82.3 %copy-start.41 = (bf16[1,1,128]{2,1,0:T(2,128)(2,1)S(1)}, bf16[1,1,128]{2,1,0:T(2,128)(2,1)}, u32[]{:S(2)}) copy-start(bf16[1,1,128]{2,1,0:T(2,128)(2,1)} %convert_bitcast_fusion.6) | copy-start | bytes 772
  341.0 98.6 %copy-start.39 = (u32[32]{0:T(128)S(1)}, u32[32]{0:T(128)}, u32[]{:S(2)}) copy-start(u32[32]{0:T(128)} %constant.81) | copy-start | bytes 388
  387.5 53.4 %collective-permute-start = (bf16[21,1024]{1,0:T(8,128)(2,1)S(1)}, bf16[21,1024]{1,0:T(8,128)(2,1)S(1)}, u32[]{:S(2)}, u32[]{:S(2)}) collective-permute-start(bf16[21,1024]{1,0:T(8,128)(2,1)S(1)} %slice), channel_id=1, source_target_pairs={{0,1},{1,2},{2,3},{4,5},{5,6},{6,7},{8,9},{9,10},{10,11},{12,13},{... | collective-permute-start | bytes 129032
  491.1 148.2 %reduce-scatter.30.cloned.1.call-start = ((), (), s32[]{:S(2)}) async-start(), calls=%async_computation.19 | async-start | bytes 10485760 | tf_op jit(solution)/shard_map/reduce_scatter | solution.py:194
  503.5 176.0 %reduce-scatter.34.cloned.1.call-start = ((), (), s32[]{:S(2)}) async-start(), calls=%async_computation.23 | async-start | bytes 73728
  511.4 230.8 %reduce-scatter.26.cloned.1.call-start = ((), (), s32[]{:S(2)}) async-start(), calls=%async_computation.17 | async-start | bytes 10485760 | tf_op jit(solution)/shard_map/reduce_scatter | solution.py:191
  524.2 338.9 %reduce-scatter.24.cloned.1.call-start = ((), (), s32[]{:S(2)}) async-start(), calls=%async_computation.16 | async-start | bytes 1179648 | tf_op jit(solution)/shard_map/reduce_scatter | solution.py:248
  553.9 322.8 %reduce-scatter.18.cloned.1.call-start = ((), (), s32[]{:S(2)}) async-start(), calls=%async_computation.13 | async-start | bytes 1179648 | tf_op jit(solution)/shard_map/reduce_scatter | solution.py:245
  617.8 325.1 %reduce-scatter.20.cloned.1.call-start = ((), (), s32[]{:S(2)}) async-start(), calls=%async_computation.14 | async-start | bytes 1179648 | tf_op jit(solution)/shard_map/reduce_scatter | solution.py:246
  629.6 380.3 %reduce-scatter.22.cloned.1.call-start = ((), (), s32[]{:S(2)}) async-start(), calls=%async_computation.15 | async-start | bytes 1179648 | tf_op jit(solution)/shard_map/reduce_scatter | solution.py:247
  639.2 462.0 %reduce-scatter.32.cloned.1.call-start = ((), (), s32[]{:S(2)}) async-start(), calls=%async_computation.20 | async-start | bytes 4718592 | tf_op jit(solution)/shard_map/reduce_scatter | solution.py:250
  643.5 549.9 %reduce-scatter.28.cloned.1.call-start = ((), (), s32[]{:S(2)}) async-start(), calls=%async_computation.18 | async-start | bytes 4718592 | tf_op jit(solution)/shard_map/reduce_scatter | solution.py:249
  755.8 49.6 %copy-start.6 = (bf16[4,577,4,64]{1,3,2,0:T(8,128)(2,1)S(1)}, bf16[4,577,4,64]{1,3,2,0:T(8,128)(2,1)}, u32[]{:S(2)}) copy-start(bf16[4,577,4,64]{1,3,2,0:T(8,128)(2,1)} %get-tuple-element.101) | copy-start | bytes 3545092
  802.3 3.5 collective-permute-start.1
  (38 other events, 358.2 us)
Sparse Core Ops, SparseCore 0:
  10.7 52.1 all-gather.17
  65.6 49.6 all-gather.21
  117.4 36.1 all-gather.25
  155.0 58.2 all-gather.19
  255.6 55.8 all-gather.23
  491.3 37.4 all-gather.27
  531.3 71.7 reduce-scatter.29
  607.4 61.2 reduce-scatter.33
  671.5 70.6 reduce-scatter.25
  746.0 63.8 reduce-scatter.23
  814.4 62.3 reduce-scatter.17
  880.6 62.3 reduce-scatter.19
  947.3 62.5 reduce-scatter.21
  1013.9 87.2 reduce-scatter.31
  1105.7 87.6 reduce-scatter.27
where the time goes:
time: 1210 us; the launch traced here: 1200 us
  blocking collectives  441 us (36%)
  waiting for transfers between devices  406 us (34%)
  matrix products  191 us (16%)
  local copies, waits for them, and re-layouts  99.4 us (8%)
  other arithmetic  42.3 us (3%)
  between operations  17.8 us (1%)
    unnamed x4, blocking collectives  135 us
    reduce_scatter x1, waiting for transfers between devices, on_device(): lax.psum_scatter(grad_up_w, 'dp', scatter_dimension=0, tiled=True)  92.2 us
    reduce_scatter x1, waiting for transfers between devices, on_device(): lax.psum_scatter(grad_down_w, 'dp', scatter_dimension=1, tiled=True)  91.4 us
    reduce_scatter x1, waiting for transfers between devices, on_device(): lax.psum_scatter(grad_value_w, 'dp', scatter_dimension=0, tiled=True)  66.9 us
    reduce_scatter x1, waiting for transfers between devices, on_device(): lax.psum_scatter(grad_key_w, 'dp', scatter_dimension=0, tiled=True)  66.2 us
    reduce_scatter x1, waiting for transfers between devices, on_device(): lax.psum_scatter(whole_up_grad.astype(jnp.bfloat16), 'tensor', scatter_di...  61.3 us
    unnamed x117, local copies, waits for them, and re-layouts  35.2 us
    all_gather x1, blocking collectives, on_device(): lax.all_gather(key_weight.astype(jnp.bfloat16), 'dp', axis=0, tiled=True)  31.4 us
  transfers between devices with their start and end apart: 17, of which 8 were waited for; matrix products, arithmetic and copies ran while one was open for 33% of the time, Pallas kernels for 0%

commit v1 on v0

v1 whole, which is shorter than its diff:
```python
import functools
import math

import jax
import jax.numpy as jnp
from jax import lax
from jax.experimental import pallas as pl
from jax.experimental.pallas import tpu as pltpu
from jax.sharding import PartitionSpec as P

HD = 64
EPS = 1e-05
SLOPE = 1.702
MESH = pl.DeviceIdType.MESH
BF = jnp.bfloat16
F32 = jnp.float32


def coords(zs):
    dp, tn = lax.axis_index("dp"), lax.axis_index("tensor")
    z, y = dp // 2, dp % 2
    x, c = tn // 2, tn % 2
    over_y = (dp + 1 - 2 * y, tn)
    over_x = (dp, tn + 2 - 4 * x)
    first = (dp + (1 - c) * (1 - 2 * y), tn + c * (2 - 4 * x))
    second = (dp + c * (1 - 2 * y), tn + (1 - c) * (2 - 4 * x))
    sibling = (dp, tn + 1 - 2 * c)
    del over_y, over_x
    fx, fy = x + c * (1 - 2 * x), y + (1 - c) * (1 - 2 * y)
    sx, sy = x + (1 - c) * (1 - 2 * x), y + c * (1 - 2 * y)
    return dict(
        dp=dp, tn=tn, z=z, y=y, x=x, c=c, first=first, second=second, sibling=sibling,
        fx=fx, fy=fy, sx=sx, sy=sy, zs=zs,
    )


def z_peer(at, step):
    return (lax.rem(at["z"] + step, at["zs"]) * 2 + at["y"], at["tn"])


def enter(at):
    barrier = pltpu.get_barrier_semaphore()
    peers = [at["first"], at["second"], at["sibling"]]
    for peer in peers:
        pl.semaphore_signal(barrier, inc=1, device_id=peer, device_id_type=MESH)

    @pl.loop(1, at["zs"])
    def _(step):
        pl.semaphore_signal(barrier, inc=1, device_id=z_peer(at, step), device_id_type=MESH)

    pl.semaphore_wait(barrier, len(peers) + at["zs"] - 1)


def remote(src, dst, send, recv, peer):
    return pltpu.make_async_remote_copy(
        src_ref=src, dst_ref=dst, send_sem=send, recv_sem=recv, device_id=peer, device_id_type=MESH
    )


class Gather:
    def __init__(self, at, own, bufs, local, zsend, zrecv, psend, precv):
        self.at, self.own, self.bufs = at, own, bufs
        self.local, self.zsend, self.zrecv, self.psend, self.precv = local, zsend, zrecv, psend, precv

    def line(self, k, x, c, y):
        return self.bufs[k].at[x, c, :, y]

    def place(self, k):
        at = self.at
        return pltpu.make_async_copy(
            self.own[k], self.bufs[k].at[at["x"], at["c"], at["z"], at["y"]], self.local.at[k]
        )

    def along_z(self, k, step, source):
        at = self.at
        return remote(
            self.own[k],
            self.bufs[k].at[at["x"], at["c"], source, at["y"]],
            self.zsend.at[k, step],
            self.zrecv.at[k, step],
            z_peer(at, step),
        )

    def to(self, k, kind):
        at = self.at
        x, y, c = at["x"], at["y"], at["c"]
        lines = [(x, y), (x, y), (at["fx"], at["fy"]), (x, y), (at["fx"], at["fy"]), (at["sx"], at["sy"]), (1 - x, 1 - y)]
        peer = [at["first"], at["second"], at["second"]] + [at["sibling"]] * 4
        lx, ly = lines[kind]
        ref = self.line(k, lx, c, ly)
        return remote(ref, ref, self.psend.at[k, kind], self.precv.at[k, kind], peer[kind])

    def start(self, k):
        self.place(k).start()

        @pl.loop(1, self.at["zs"])
        def _(step):
            self.along_z(k, step, self.at["z"]).start()

    def after_z(self, k):
        at = self.at
        self.place(k).wait()

        @pl.loop(1, at["zs"])
        def _(step):
            self.along_z(k, step, lax.rem(at["z"] - step + at["zs"], at["zs"])).wait_recv()

        for kind in (0, 1, 3):
            self.to(k, kind).start()

    def wait(self, k, kind):
        at = self.at
        ref = self.line(k, at["x"], at["c"], at["y"])
        x, y, c = at["x"], at["y"], at["c"]
        got = [
            (at["fx"], c, at["fy"]),
            (at["sx"], c, at["sy"]),
            (1 - x, c, 1 - y),
            (x, 1 - c, y),
            (at["sx"], 1 - c, at["sy"]),
            (at["fx"], 1 - c, at["fy"]),
            (1 - x, 1 - c, 1 - y),
        ][kind]
        ref = self.line(k, *got)
        remote(ref, ref, self.psend.at[k, kind], self.precv.at[k, kind], at["sibling"]).wait_recv()

    def after_first(self, k):
        self.wait(k, 0)
        self.to(k, 2).start()
        self.to(k, 4).start()

    def after_second(self, k):
        self.wait(k, 1)
        self.to(k, 5).start()
        self.wait(k, 2)
        self.to(k, 6).start()

    def done(self, k):
        for kind in (3, 4, 5, 6):
            self.wait(k, kind)

    def drain(self, k):
        @pl.loop(1, self.at["zs"])
        def _(step):
            self.along_z(k, step, self.at["z"]).wait_send()

        for kind in range(7):
            self.to(k, kind).wait_send()


def gather_kernel(n, zs, *refs):
    own, bufs, sems = refs[:n], refs[n : 2 * n], refs[2 * n :]
    at = coords(zs)
    enter(at)
    g = Gather(at, own, bufs, *sems)
    for k in range(n):
        g.start(k)
    for k in range(n + 2):
        if k < n:
            g.after_z(k)
        if 0 <= k - 1 < n:
            g.after_first(k - 1)
        if 0 <= k - 2 < n:
            g.after_second(k - 2)
    for k in range(n):
        g.done(k)
    for k in range(n):
        g.drain(k)


def gather(own, zs):
    n = len(own)
    return pl.pallas_call(
        functools.partial(gather_kernel, n, zs),
        out_shape=[jax.ShapeDtypeStruct((2, 2, zs, 2) + b.shape, b.dtype) for b in own],
        in_specs=[pl.BlockSpec(memory_space=pl.ANY)] * n,
        out_specs=[pl.BlockSpec(memory_space=pl.ANY)] * n,
        scratch_shapes=[
            pltpu.SemaphoreType.DMA((n,)),
            pltpu.SemaphoreType.DMA((n, zs)),
            pltpu.SemaphoreType.DMA((n, zs)),
            pltpu.SemaphoreType.DMA((n, 7)),
            pltpu.SemaphoreType.DMA((n, 7)),
        ],
        compiler_params=pltpu.CompilerParams(collective_id=0, has_side_effects=True),
        name="gather_weights",
    )(*own)


def scatter_kernel(n, zs, *refs):
    parts, outs = refs[:n], refs[n : 2 * n]
    refs = refs[2 * n :]
    kept, rc, rs, rz = refs[:n], refs[n : 2 * n], refs[2 * n : 3 * n], refs[3 * n : 4 * n]
    local, zsend, zrecv, psend, precv = refs[4 * n :]
    at = coords(zs)
    x, y, c, z = at["x"], at["y"], at["c"], at["z"]
    enter(at)

    def keep(k):
        return pltpu.make_async_copy(parts[k].at[:, c], kept[k], local.at[k])

    def to_sibling(k):
        return remote(parts[k].at[:, 1 - c], rc[k], psend.at[k, 0], precv.at[k, 0], at["sibling"])

    def to_second(k, which):
        lx, ly = ((at["sx"], at["sy"]), (1 - x, 1 - y))[which]
        return remote(
            kept[k].at[lx, :, ly], rs[k].at[which], psend.at[k, 1 + which], precv.at[k, 1 + which], at["second"]
        )

    def to_first(k):
        return remote(kept[k].at[at["fx"], :, at["fy"]], rs[k].at[2], psend.at[k, 3], precv.at[k, 3], at["first"])

    def along_z(k, step):
        return remote(
            kept[k].at[x, lax.rem(z + step, zs), y], rz[k].at[step], zsend.at[k, step], zrecv.at[k, step], z_peer(at, step)
        )

    def add(dst, src):
        dst[...] = (dst[...].astype(F32) + src[...].astype(F32)).astype(dst.dtype)

    def stage0(k):
        to_sibling(k).start()
        keep(k).start()

    def stage1(k):
        to_sibling(k).wait_recv()
        keep(k).wait()

        for which, (lx, ly) in enumerate(
            ((1 - x, 1 - y), (at["sx"], at["sy"]), (at["fx"], at["fy"]), (x, y))
        ):

            @pl.loop(0, zs)
            def _(i):
                add(kept[k].at[lx, i, ly], rc[k].at[lx, i, ly])

            if which == 0:
                to_second(k, 1).start()
            elif which == 1:
                to_second(k, 0).start()

    def stage2(k):
        to_second(k, 1).wait_recv()

        @pl.loop(0, zs)
        def _(i):
            add(kept[k].at[at["fx"], i, at["fy"]], rs[k].at[1, i])

        to_first(k).start()
        to_second(k, 0).wait_recv()

        @pl.loop(0, zs)
        def _(i):
            add(kept[k].at[x, i, y], rs[k].at[0, i])

    def stage3(k):
        to_first(k).wait_recv()

        @pl.loop(0, zs)
        def _(i):
            add(kept[k].at[x, i, y], rs[k].at[2, i])

        @pl.loop(1, zs)
        def _(step):
            along_z(k, step).start()

    def stage4(k):
        outs[k][...] = kept[k][x, z, y].astype(F32)

        @pl.loop(1, zs)
        def _(step):
            along_z(k, step).wait_recv()
            outs[k][...] += rz[k][step].astype(F32)

    stages = (stage0, stage1, stage2, stage3, stage4)
    for tick in range(n + len(stages) - 1):
        for late, stage in enumerate(stages):
            if 0 <= tick - late < n:
                stage(tick - late)
    for k in range(n):
        to_sibling(k).wait_send()
        to_second(k, 0).wait_send()
        to_second(k, 1).wait_send()
        to_first(k).wait_send()

        @pl.loop(1, zs)
        def _(step):
            along_z(k, step).wait_send()


def scatter(parts, zs):
    n = len(parts)
    blocks = [p.shape[4:] for p in parts]
    return pl.pallas_call(
        functools.partial(scatter_kernel, n, zs),
        out_shape=[jax.ShapeDtypeStruct(b, F32) for b in blocks],
        in_specs=[pl.BlockSpec(memory_space=pl.ANY)] * n,
        out_specs=[pl.BlockSpec(memory_space=pltpu.VMEM)] * n,
        scratch_shapes=[pltpu.VMEM((2, zs, 2) + b, p.dtype) for b, p in zip(blocks, parts)]
        + [pltpu.VMEM((2, zs, 2) + b, p.dtype) for b, p in zip(blocks, parts)]
        + [pltpu.VMEM((3, zs) + b, p.dtype) for b, p in zip(blocks, parts)]
        + [pltpu.VMEM((zs,) + b, p.dtype) for b, p in zip(blocks, parts)]
        + [
            pltpu.SemaphoreType.DMA((n,)),
            pltpu.SemaphoreType.DMA((n, zs)),
            pltpu.SemaphoreType.DMA((n, zs)),
            pltpu.SemaphoreType.DMA((n, 4)),
            pltpu.SemaphoreType.DMA((n, 4)),
        ],
        compiler_params=pltpu.CompilerParams(
            collective_id=1, has_side_effects=True, vmem_limit_bytes=52 * 1024 * 1024
        ),
        name="scatter_grads",
    )(*parts)


def normalize(values, gain, shift):
    centre = values - jnp.mean(values, axis=-1, keepdims=True)
    inverse = lax.rsqrt(jnp.mean(centre * centre, axis=-1, keepdims=True) + EPS)
    normed = centre * inverse
    return (normed * gain + shift, normed, inverse)


def normalize_back(grad_out, normed, inverse, gain):
    scaled = grad_out * gain
    grad_in = inverse * (
        scaled
        - jnp.mean(scaled, axis=-1, keepdims=True)
        - normed * jnp.mean(scaled * normed, axis=-1, keepdims=True)
    )
    return (grad_in, jnp.sum(grad_out * normed, axis=0), jnp.sum(grad_out, axis=0))


def attend(query, key, value):
    scale = 1.0 / math.sqrt(query.shape[-1])
    scores = jnp.einsum("qhd,khd->hqk", query, key, preferred_element_type=F32) * scale
    highest = jnp.max(scores, axis=-1, keepdims=True)
    expo = jnp.exp(scores - highest)
    total = jnp.sum(expo, axis=-1, keepdims=True)
    probs = (expo / total).astype(BF)
    mixed = jnp.einsum("hqk,khd->qhd", probs, value, preferred_element_type=F32)
    return (mixed.astype(BF), (highest + jnp.log(total))[..., 0])


def attend_back(query, key, value, grad_mixed, log_total):
    scale = 1.0 / math.sqrt(query.shape[-1])
    scores = jnp.einsum("qhd,khd->hqk", query, key, preferred_element_type=F32) * scale
    probs = jnp.exp(scores - log_total[..., None])
    grad_value = jnp.einsum(
        "hqk,qhd->khd", probs.astype(BF), grad_mixed, preferred_element_type=F32
    ).astype(BF)
    grad_probs = jnp.einsum("qhd,khd->hqk", grad_mixed, value, preferred_element_type=F32)
    grad_scores = probs * (grad_probs - jnp.sum(grad_probs * probs, axis=-1, keepdims=True))
    grad_scores = grad_scores.astype(BF)
    grad_query = jnp.einsum("hqk,khd->qhd", grad_scores, key, preferred_element_type=F32) * scale
    grad_key = jnp.einsum("hqk,qhd->khd", grad_scores, query, preferred_element_type=F32) * scale
    return (grad_query.astype(BF), grad_key.astype(BF), grad_value)


def on_device(
    tokens,
    cotangent,
    image_mask,
    query_weight,
    key_weight,
    value_weight,
    out_weight,
    up_weight,
    down_weight,
    query_bias,
    value_bias,
    up_bias,
    attn_gain,
    attn_shift,
    mlp_gain,
    mlp_shift,
    out_bias,
    down_bias,
):
    rows, dim = tokens.shape
    dps, tns = lax.axis_size("dp"), lax.axis_size("tensor")
    zs = dps // 2
    hw = query_weight.shape[1]
    half = up_weight.shape[1] // 2
    low_up, low_down = up_weight.astype(BF), down_weight.astype(BF).T
    small = jnp.concatenate(
        [query_bias.reshape(-1), value_bias.reshape(-1), up_bias.reshape(-1)]
        + [attn_gain, attn_shift, mlp_gain, mlp_shift, out_bias, down_bias]
    ).astype(BF)
    n_small = small.shape[0]
    pad = -(-n_small // 2048) * 2048
    own = [
        jnp.pad(small, (0, pad - n_small)).reshape(-1, 128),
        jnp.concatenate([query_weight.astype(BF), key_weight.astype(BF)], axis=1),
        jnp.concatenate([value_weight.astype(BF), out_weight.astype(BF).T], axis=1),
        low_up[:, :half],
        low_up[:, half:],
        low_down[:, :half],
        low_down[:, half:],
    ]
    got = gather(own, zs)
    vecs = got[0].reshape(tns, dps, pad).astype(F32)
    heads_t = query_bias.shape[0]
    q_b, v_b, u_b = query_bias.size, value_bias.size, up_bias.size
    vec_query = vecs[:, :, :q_b].reshape(tns, dps, heads_t, -1).transpose(0, 2, 1, 3).reshape(-1)
    vec_value = vecs[:, :, q_b : q_b + v_b].reshape(tns, dps, heads_t, -1).transpose(0, 2, 1, 3).reshape(-1)
    at_u = q_b + v_b
    vec_up = (
        vecs[:, :, at_u : at_u + u_b].reshape(tns, dps, up_bias.shape[0], -1).transpose(0, 2, 1, 3).reshape(-1)
    )
    at_d = at_u + u_b
    own_d = attn_gain.shape[0]
    gain_a, shift_a, gain_m, shift_m, vec_out, vec_down = (
        vecs[0, :, at_d + i * own_d : at_d + (i + 1) * own_d].reshape(-1) for i in range(6)
    )
    mats = [g.reshape(tns, dim, -1) for g in got[1:]]

    def whole(pieces):
        return jnp.concatenate(pieces, axis=2).transpose(1, 0, 2).reshape(dim, -1)

    full_query, full_key = whole([mats[0][:, :, :hw]]), whole([mats[0][:, :, hw:]])
    full_value, full_out_t = whole([mats[1][:, :, :hw]]), whole([mats[1][:, :, hw:]])
    whole_up, whole_down_t = whole(mats[2:4]), whole(mats[4:6])

    image = lax.axis_index("tensor")
    row_mask = image_mask[image].astype(F32)
    inputs = tokens.astype(F32)
    normed_a, unit_a, inverse_a = normalize(inputs, gain_a, shift_a)
    attn_in = normed_a.astype(BF)
    query = (jnp.dot(attn_in, full_query, preferred_element_type=F32) + vec_query).astype(BF)
    key = jnp.dot(attn_in, full_key, preferred_element_type=F32).astype(BF)
    value = (jnp.dot(attn_in, full_value, preferred_element_type=F32) + vec_value).astype(BF)
    shaped = (rows, -1, HD)
    q3, k3, v3 = query.reshape(shaped), key.reshape(shaped), value.reshape(shaped)
    mixed3, log_total = attend(q3, k3, v3)
    mixed = mixed3.reshape(rows, dim)
    middle = inputs + jnp.einsum("rh,dh->rd", mixed, full_out_t, preferred_element_type=F32) + vec_out
    normed_m, unit_m, inverse_m = normalize(middle, gain_m, shift_m)
    grad_out = cotangent.astype(F32) * row_mask
    grad_down_b = jnp.sum(grad_out, axis=0)
    mlp_in = normed_m.astype(BF)
    pre = jnp.dot(mlp_in, whole_up, preferred_element_type=F32) + vec_up
    sigma = jax.nn.sigmoid(SLOPE * pre)
    hidden = (pre * sigma).astype(BF)
    branch = jnp.einsum("rf,df->rd", hidden, whole_down_t, preferred_element_type=F32)
    block_out = ((middle + branch + vec_down) * row_mask).astype(BF)
    grad_branch = grad_out.astype(BF)
    down_t_grad = jnp.einsum("rd,rf->df", grad_branch, hidden, preferred_element_type=F32).astype(BF)
    grad_hidden = jnp.dot(grad_branch, whole_down_t, preferred_element_type=F32)
    grad_pre = (grad_hidden * (sigma + SLOPE * pre * sigma * (1.0 - sigma))).astype(BF)
    up_b_grad = jnp.sum(grad_pre.astype(F32), axis=0)
    up_grad = jnp.einsum("rd,rf->df", mlp_in, grad_pre, preferred_element_type=F32).astype(BF)
    grad_normed_m = jnp.einsum("rf,df->rd", grad_pre, whole_up, preferred_element_type=F32)
    grad_mid_norm, grad_gain_m, grad_shift_m = normalize_back(grad_normed_m, unit_m, inverse_m, gain_m)
    grad_middle = grad_out + grad_mid_norm
    grad_out_b = jnp.sum(grad_middle, axis=0)
    grad_attn = grad_middle.astype(BF)
    out_t_grad = jnp.einsum("rd,rh->dh", grad_attn, mixed, preferred_element_type=F32).astype(BF)
    grad_mixed = jnp.dot(grad_attn, full_out_t, preferred_element_type=F32).astype(BF)
    gq3, gk3, gv3 = attend_back(q3, k3, v3, grad_mixed.reshape(shaped), log_total)
    grad_query, grad_key, grad_value = gq3.reshape(rows, dim), gk3.reshape(rows, dim), gv3.reshape(rows, dim)
    query_grad = jnp.einsum("rd,rh->dh", attn_in, grad_query, preferred_element_type=F32).astype(BF)
    key_grad = jnp.einsum("rd,rh->dh", attn_in, grad_key, preferred_element_type=F32).astype(BF)
    value_grad = jnp.einsum("rd,rh->dh", attn_in, grad_value, preferred_element_type=F32).astype(BF)
    query_b_grad = jnp.sum(grad_query.astype(F32), axis=0)
    value_b_grad = jnp.sum(grad_value.astype(F32), axis=0)
    grad_normed_a = (
        jnp.einsum("rh,dh->rd", grad_query, full_query, preferred_element_type=F32)
        + jnp.einsum("rh,dh->rd", grad_key, full_key, preferred_element_type=F32)
        + jnp.einsum("rh,dh->rd", grad_value, full_value, preferred_element_type=F32)
    )
    grad_in_norm, grad_gain_a, grad_shift_a = normalize_back(grad_normed_a, unit_a, inverse_a, gain_a)
    tokens_grad = grad_middle + grad_in_norm

    def blocks(mat):
        return mat.reshape(dim, tns, -1).transpose(1, 0, 2)

    def frame(mat, width):
        return mat.reshape(2, 2, zs, 2, -1, width)

    def spread(vec, lead):
        return vec.reshape(tns, lead, dps, -1).transpose(0, 2, 1, 3).reshape(tns, dps, -1)

    small_d = jnp.concatenate(
        [
            v.reshape(dps, -1)
            for v in (grad_gain_a, grad_shift_a, grad_gain_m, grad_shift_m, grad_out_b, grad_down_b)
        ],
        axis=1,
    )
    small_grad = jnp.concatenate(
        [
            spread(query_b_grad, heads_t),
            spread(value_b_grad, heads_t),
            spread(up_b_grad, up_bias.shape[0]),
            jnp.broadcast_to(small_d, (tns,) + small_d.shape),
        ],
        axis=2,
    )
    small_grad = jnp.pad(small_grad, ((0, 0), (0, 0), (0, pad - n_small)))
    up_blocks, down_blocks = blocks(up_grad), blocks(down_t_grad)
    parts = [
        frame(down_blocks[:, :, :half], half),
        frame(down_blocks[:, :, half:], half),
        frame(up_blocks[:, :, :half], half),
        frame(up_blocks[:, :, half:], half),
        frame(jnp.concatenate([blocks(value_grad), blocks(out_t_grad)], axis=2), 2 * hw),
        frame(jnp.concatenate([blocks(query_grad), blocks(key_grad)], axis=2), 2 * hw),
        frame(small_grad, 128),
    ]
    down0, down1, up0, up1, vo, qk, sm = scatter(parts, zs)
    sm = sm.reshape(-1)
    return (
        block_out,
        tokens_grad,
        qk[:, :hw],
        qk[:, hw:],
        vo[:, :hw],
        vo[:, hw:].T,
        jnp.concatenate([up0, up1], axis=1),
        jnp.concatenate([down0, down1], axis=1).T,
        sm[:q_b].reshape(query_bias.shape),
        sm[q_b : q_b + v_b].reshape(value_bias.shape),
        sm[at_u : at_u + u_b].reshape(up_bias.shape),
    ) + tuple(sm[at_d + i * own_d : at_d + (i + 1) * own_d] for i in range(6))


def solution(mesh):
    wide, tall = P("dp", "tensor"), P("tensor", "dp")
    rows = P(("dp", "tensor"), None)
    weights = (wide, wide, wide, tall, wide, tall, tall, tall, tall)
    vectors = (P("dp"),) * 6
    return jax.shard_map(
        on_device,
        mesh=mesh,
        in_specs=(rows, rows, P("dp")) + weights + vectors,
        out_specs=(rows, rows) + weights + vectors,
        check_vma=False,
    )
```

time: 1210 us -> 638 us (0.53)
  blocking collectives: 441 us -> 0 us
  waiting for transfers between devices: 406 us -> 0 us
  Pallas kernels: 0 us -> 270 us
  matrix products: 191 us -> 166 us
  local copies, waits for them, and re-layouts: 99.4 us -> 123 us
  other arithmetic: 42.3 us -> 65.2 us
  between operations: 17.8 us -> 2.52 us
    reduce_scatter x8 -> x0, waiting for transfers between devices: 392 us -> none  [the longest x1 92.2 us: on_device(): lax.psum_scatter(grad_up_w, 'dp', scatter_dimension=0, tiled=True)]
    all_gather x14 -> x0, blocking collectives: 298 us -> none  [the longest x1 31.4 us: on_device(): lax.all_gather(key_weight.astype(jnp.bfloat16), 'dp', axis=0, tiled=True)]
    pallas_call x0 -> x2, Pallas kernels: none -> 270 us  [the longest x1 142 us: scatter(): pl.pallas_call(functools.partial(scatter_kernel, n, zs), out_shape=[jax.S...]
    unnamed x4 -> x0, blocking collectives: 135 us -> none
    reshape x8 -> x23, local copies, waits for them, and re-layouts: 29.9 us -> 59.4 us  [the longest x6 29.8 us: blocks(): return mat.reshape(dim, tns, -1).transpose(1, 0, 2)]
    while x16 -> x0, local copies, waits for them, and re-layouts: 28.5 us -> none  [the longest x4 15.1 us: on_device(): lax.map(attend_image, (query_img, key_img, value_img))]
    concatenate x0 -> x6, other arithmetic: none -> 25 us  [the longest x2 15.6 us: whole(): return jnp.concatenate(pieces, axis=2).transpose(1, 0, 2).reshape(dim, -1)]
    dot_general x46 -> x24, matrix products: 191 us -> 166 us  [the longest x1 15.1 us: attend_back(): jnp.einsum('qhd,khd->hqk', grad_mixed, value, preferred_element_type=F32)]
  transfers between devices with their start and end apart: 17 -> 0, of which waited for: 8 -> 0; matrix products, arithmetic and copies ran while one was open for 33% -> 0% of each run, Pallas kernels for 0% -> 0%
where the time goes in v1:
time: 638 us; the launch traced here: 628 us
  Pallas kernels  270 us (42%)
  matrix products  166 us (26%)
  local copies, waits for them, and re-layouts  123 us (19%)
  other arithmetic  65.2 us (10%)
    pallas_call x1, Pallas kernels, scatter(): pl.pallas_call(functools.partial(scatter_kernel, n, zs), out_shape=[jax.S...  142 us
    pallas_call x1, Pallas kernels, gather(): pl.pallas_call(functools.partial(gather_kernel, n, zs), out_shape=[jax.Sh...  129 us
    reshape x6, local copies, waits for them, and re-layouts, blocks(): return mat.reshape(dim, tns, -1).transpose(1, 0, 2)  29.8 us
    reshape x4, local copies, waits for them, and re-layouts, on_device(): mats = [g.reshape(tns, dim, -1) for g in got[1:]]  25.2 us
    unnamed x126, local copies, waits for them, and re-layouts  24.1 us
    convert_element_type x1, other arithmetic, attend_back(): grad_scores = grad_scores.astype(BF)  16.1 us
    concatenate x2, other arithmetic, whole(): return jnp.concatenate(pieces, axis=2).transpose(1, 0, 2).reshape(dim, -1)  15.6 us
    dot_general x1, matrix products, attend_back(): jnp.einsum('qhd,khd->hqk', grad_mixed, value, preferred_element_type=F32)  15.1 us

profile of v1, /device:TPU:0, one launch (start us, length us, event | category | flops | bytes accessed | tf_op | source)
XLA Modules:
  0.0 627.9 jit_solution(10839068015337883045)
XLA Ops:
  14.2 128.7 %gather_weights.1 = (bf16[2,2,4,2,16,128]{5,4,3,2,1,0:T(8,128)(2,1)}, bf16[2,2,4,2,128,512]{5,4,3,2,1,0:T(8,128)(2,1)}, bf16[2,2,4,2,128,512]{5,4,3,2,1,0:T(8,12...) custom-call(bf16[16,128]{1,0:T(8,128)(2,1)} %pad_bitcast_fusion.refs, ...), custom_call_target="tpu_custom_call" | custom-call | tf_op jit(solution)/shard_map/gather_weights/pallas_call | solution.py:173
  162.5 4.5 fusion.46
  179.7 4.4 copy.121
  184.1 4.3 convolution_convert_fusion.7
  190.2 10.0 %multiply_reduce_fusion.1 = (f32[16,577]{1,0:T(8,128)S(1)}, f32[16,577,577]{1,2,0:T(8,128)}) fusion(bf16[577,16,64]{0,2,1:T(8,128)(2,1)S(1)} %bitcast.175, bf16[577,16,64]{0,2,1:T(8,128)(2,1)S(1)} %bitcast.171), kind=kOutput, calls=%fused_computation.6 | convolution fusion | flops 692483072 | bytes 23707776 | tf_op jit(solution)/shard_map/qhd,khd->hqk/dot_general | solution.py:337
  200.1 10.5 %fusion = f32[16,577]{1,0:T(8,128)S(1)} fusion(f32[16,577,577]{1,2,0:T(8,128)} %get-tuple-element.140, f32[16,577]{1,0:T(8,128)S(1)} %get-tuple-element.139), kind=kLoop, calls=%fused_computation.5 | loop fusion | flops 15971360 | bytes 21381312 | tf_op jit(solution)/shard_map/reduce_sum | solution.py:340
  210.7 11.7 %fusion.27 = bf16[16,64,577]{2,1,0:T(8,128)(2,1)} fusion(bf16[577,16,64]{0,2,1:T(8,128)(2,1)S(1)} %bitcast.193, f32[16,577,577]{1,2,0:T(8,128)} %get-tuple-element.140, f32[16,577]{1,0:T(8,128)S(1)} %fusion, f32[16,577]{1,0:T(8,128)S(1)} %get-tuple-element.139), kind=kOutput, calls=%fused_computation.66 | convolution fusion | flops 703736896 | bytes 23744704 | tf_op jit(solution)/shard_map/hqk,khd->qhd/dot_general | solution.py:342
  224.9 4.9 fusion.53
  229.8 6.3 %copy.99 = bf16[4,1024,512]{1,2,0:T(8,128)(2,1)} copy(bf16[4,1024,512]{2,1,0:T(8,128)(2,1)} %bitcast.200) | data formatting | bytes 8388608 | tf_op jit(solution)/shard_map/reshape | solution.py:417
  236.1 6.3 %copy.98 = bf16[4,1024,512]{1,2,0:T(8,128)(2,1)} copy(bf16[4,1024,512]{2,1,0:T(8,128)(2,1)} %bitcast.199) | data formatting | bytes 8388608 | tf_op jit(solution)/shard_map/reshape | solution.py:417
  242.3 7.8 %pad_maximum_fusion.1 = bf16[4,1024,1024]{1,2,0:T(8,128)(2,1)} fusion(bf16[4,1024,512]{1,2,0:T(8,128)(2,1)} %copy.99, bf16[4,1024,512]{1,2,0:T(8,128)(2,1)} %copy.98), kind=kLoop, calls=%fused_computation.19 | loop fusion | flops 16777216 | bytes 16777216 | tf_op jit(solution)/shard_map/concatenate | solution.py:420
  251.4 6.3 %copy.96 = bf16[4,1024,512]{1,2,0:T(8,128)(2,1)} copy(bf16[4,1024,512]{2,1,0:T(8,128)(2,1)} %bitcast.198) | data formatting | bytes 8388608 | tf_op jit(solution)/shard_map/reshape | solution.py:417
  257.7 6.3 copy.95
  264.0 7.8 %pad_maximum_fusion = bf16[4,1024,1024]{1,2,0:T(8,128)(2,1)} fusion(bf16[4,1024,512]{1,2,0:T(8,128)(2,1)} %copy.96, bf16[4,1024,512]{1,2,0:T(8,128)(2,1)} %copy.95), kind=kLoop, calls=%fused_computation.18 | loop fusion | flops 16777216 | bytes 16777216 | tf_op jit(solution)/shard_map/concatenate | solution.py:420
  272.5 11.5 %fusion.35 = f32[577,4096]{1,0:T(8,128)} fusion(bf16[1024,4096]{0,1:T(8,128)(2,1)} %bitcast.183, f32[577,1024]{1,0:T(8,128)S(1)} %copy-done.8, f32[1024]{0:T(1024)S(1)} %copy-done.47, f32[1024]{0:T(1024)S(1)} %copy-done.40, f32[577]{0:T(1024)S(1)} %add_rsqrt_fusion, f32[577]{0:T(1024)S(1)} %broadcast_multiply_fusion.4), kind=kOutput, calls=%fused_computation.107 | convolution fusion | flops 4843181056 | bytes 20218376 | tf_op jit(solution)/shard_map/dot_general | solution.py:443
  284.3 12.5 %multiply_convert_fusion.5 = bf16[577,1024]{1,0:T(8,128)(2,1)} fusion(f32[577,1024]{1,0:T(8,128)S(1)} %copy-done.8, bf16[1024,4096]{0,1:T(8,128)(2,1)} %bitcast.181, f32[]{:T(128)} %bitcast.35, f32[1024]{0:T(1024)S(1)} %copy-done.49, f32[577,4096]{1,0:T(8,128)} %fusion.35, f32[4096]{0:T(1024)S(1)} %add.143), kind=kOutput, calls=%fused_computation.53 | convolution fusion | flops 4859133952 | bytes 21407748 | tf_op jit(solution)/shard_map/rf,df->rd/dot_general | solution.py:446
  296.8 15.1 %convert_reduce_fusion = (f32[4096]{0:T(1024)S(1)}, bf16[577,4096]{1,0:T(8,128)(2,1)}) fusion(f32[577,4096]{1,0:T(8,128)} %fusion.35, f32[4096]{0:T(1024)S(1)} %add.143, bf16[1024,4096]{0,1:T(8,128)(2,1)} %bitcast.182, bf16[577,1024]{1,0:T(8,128)(2,1)S(1)} %copy-done.27, f32[]{:T(128)} %bitcast.35), kind=kOutput, calls=%fused_computation.12 | convolution fusion | flops 4872719360 | bytes 23783428 | tf_op jit(solution)/shard_map/dot_general | solution.py:450
  311.9 8.1 %multiply_reduce_fusion.2 = (f32[1024]{0:T(1024)S(1)}, f32[577]{0:T(1024)S(1)}, f32[577]{0:T(1024)S(1)}, f32[1024]{0:T(1024)S(1)}, f32[577,1024]{1,0:T(8,128)S(1)}) fusion(f32[577,1024]{1,0:T(8,128)S(1)} %copy-done.8, f32[577]{0:T(1024)S(1)} %add_rsqrt_fusion, f32[577]{0:T(1024)S(1)} %broadcast_multiply_fusion.4, f32[1024]{0:T(1024)S(1)} %copy-done.40, ...), kind=kOutput, calls=%fused_computation.46 | convolution fusion | flops 4845541376 | bytes 17863696 | tf_op jit(solution)/shard_map/rf,df->rd/dot_general | solution.py:454
  325.0 11.3 %convert_reduce_fusion.2 = (f32[16,64]{1,0:T(8,128)S(1)}, bf16[16,64,577]{2,1,0:T(8,128)(2,1)}) fusion(bf16[577,16,64]{0,2,1:T(8,128)(2,1)S(1)} %bitcast.173, f32[16,577,577]{1,2,0:T(8,128)} %get-tuple-element.140, f32[16,577]{1,0:T(8,128)S(1)} %log_add_fusion), kind=kOutput, calls=%fused_computation.33 | convolution fusion | flops 699590720 | bytes 23711872 | tf_op jit(solution)/shard_map/hqk,qhd->khd/dot_general | solution.py:350
  336.3 15.1 %multiply_reduce_fusion = (f32[16,577]{1,0:T(8,128)S(1)}, f32[16,577,577]{1,2,0:T(8,128)}) fusion(f32[16,577,577]{1,2,0:T(8,128)} %get-tuple-element.140, f32[16,577]{1,0:T(8,128)S(1)} %log_add_fusion, bf16[577,16,64]{0,2,1:T(8,128)(2,1)S(1)} %bitcast.174, bf16[577,16,64]{0,2,1:T(8,128)(2,1)S(1)} %bitcast.194), kind=kOutput, calls=%fused_computation.1 | convolution fusion | flops 703136768 | bytes 45052160 | tf_op jit(solution)/shard_map/qhd,khd->hqk/dot_general | solution.py:353
  351.4 16.1 %multiply_convert_fusion = bf16[16,577,577]{1,2,0:T(8,128)(2,1)S(1)} fusion(f32[16,577,577]{1,2,0:T(8,128)} %get-tuple-element.145, f32[16,577,577]{1,2,0:T(8,128)} %get-tuple-element.140, f32[16,577]{1,0:T(8,128)S(1)} %get-tuple-element.144, f32[16,577]{1,0:T(8,128)S(1)} %log_add_fusion), kind=kLoop, calls=%fused_computation | loop fusion | flops 26634320 | bytes 53342496 | tf_op jit(solution)/shard_map/convert_element_type | solution.py:355
  376.2 8.2 %multiply_convert_fusion.3 = bf16[16,64,577]{2,1,0:T(8,128)(2,1)S(1)} fusion(bf16[577,16,64]{0,2,1:T(8,128)(2,1)S(1)} %bitcast.176, bf16[16,577,577]{1,2,0:T(8,128)(2,1)} %copy-done), kind=kOutput, calls=%fused_computation.35 | convolution fusion | flops 683020288 | bytes 13017120 | tf_op jit(solution)/shard_map/hqk,qhd->khd/dot_general | solution.py:357
  392.3 9.5 %convolution_convert_fusion.1 = bf16[1024,4096]{1,0:T(8,128)(2,1)} fusion(bf16[577,1024]{1,0:T(8,128)(2,1)S(1)} %copy-done.28, f32[]{:T(128)} %bitcast.35, f32[577,4096]{1,0:T(8,128)S(1)} %bitcast.224, f32[4096]{0:T(1024)S(1)} %add.143), kind=kOutput, calls=%fused_computation.21 | convolution fusion | flops 4862737408 | bytes 19040260 | tf_op jit(solution)/shard_map/rd,rf->df/dot_general | solution.py:449
  401.8 8.0 %copy.129 = bf16[128,4,8,1024]{3,2,0,1:T(8,128)(2,1)} copy(bf16[128,4,8,1024]{3,2,1,0:T(8,128)(2,1)} %bitcast.186) | data formatting | bytes 16777216 | tf_op jit(solution)/shard_map/reshape | solution.py:477
  409.8 6.0 fusion.44
  415.7 11.7 %convolution_convert_fusion = bf16[1024,4096]{1,0:T(8,128)(2,1)} fusion(bf16[577,4096]{1,0:T(8,128)(2,1)} %get-tuple-element.148, f32[577,1024]{1,0:T(8,128)S(1)} %copy-done.9, f32[1024]{0:T(1024)S(1)} %copy-done.48, f32[1024]{0:T(1024)S(1)} %copy-done.40, f32[577]{0:T(1024)S(1)} %add_rsqrt_fusion, f32[577]{0:T(1024)S(1)} %broadcast_multiply_fusion.4), kind=kOutput, calls=%fused_computation.20 | convolution fusion | flops 4847375360 | bytes 15491592 | tf_op jit(solution)/shard_map/rd,rf->df/dot_general | solution.py:453
  427.4 8.0 %copy.128 = bf16[128,4,8,1024]{3,2,0,1:T(8,128)(2,1)} copy(bf16[128,4,8,1024]{3,2,1,0:T(8,128)(2,1)} %bitcast.185) | data formatting | bytes 16777216 | tf_op jit(solution)/shard_map/reshape | solution.py:477
  435.4 5.8 fusion.43
  447.5 4.6 convolution_convert_fusion.5
  456.0 4.0 pad_maximum_fusion.2
  466.2 4.7 convolution_convert_fusion.3
  479.6 141.8 %scatter_grads.1 = (f32[128,512]{1,0:T(8,128)S(1)}, f32[128,512]{1,0:T(8,128)S(1)}, f32[128,512]{1,0:T(8,128)S(1)}, f32[128,512]{1,0:T(8,128)S(1)}, f32[128,512]...) custom-call(bf16[2,2,4,2,128,512]{5,4,3,2,1,0:T(8,128)(2,1)} %bitcast.168, ...), custom_call_target="tpu_custom_call" | custom-call | tf_op jit(solution)/shard_map/scatter_grads/pallas_call | solution.py:295
  (214 shorter events, 103.8 us)
Async XLA Ops:
  0.7 12.7 %copy-start.29 = (f32[128,1024]{1,0:T(8,128)S(1)}, f32[128,1024]{1,0:T(8,128)}, u32[]{:S(2)}) copy-start(f32[128,1024]{1,0:T(8,128)} %param.25) | copy-start | bytes 1572868
  148.3 7.6 %copy-start.5 = (bf16[577,1024]{1,0:T(8,128)(2,1)S(1)}, bf16[577,1024]{1,0:T(8,128)(2,1)}, u32[]{:S(2)}) copy-start(bf16[577,1024]{1,0:T(8,128)(2,1)} %param.18) | copy-start | bytes 3545092
  150.8 6.6 %copy-start.23 = (bf16[4,1024,256]{1,2,0:T(8,128)(2,1)S(1)}, bf16[4,1024,256]{1,2,0:T(8,128)(2,1)}, u32[]{:S(2)}) copy-start(bf16[4,1024,256]{1,2,0:T(8,128)(2,1)} %copy.119) | copy-start | bytes 6291460
  170.0 4.5 copy-start.12
  179.6 10.5 %copy-start.3 = (bf16[577,1024]{0,1:T(8,128)(2,1)}, bf16[577,1024]{0,1:T(8,128)(2,1)S(1)}, u32[]{:S(2)}) copy-start(bf16[577,1024]{0,1:T(8,128)(2,1)S(1)} %copy.90) | copy-start | bytes 3545092
  179.6 4.5 copy-start.35
  179.6 4.5 copy-start.38
  179.6 4.5 copy-start.42
  179.7 4.5 copy-start.45
  190.1 10.0 %copy-start.1 = (bf16[577,1024]{0,1:T(8,128)(2,1)}, bf16[577,1024]{0,1:T(8,128)(2,1)S(1)}, u32[]{:S(2)}) copy-start(bf16[577,1024]{0,1:T(8,128)(2,1)S(1)} %copy.92) | copy-start | bytes 3545092
  200.1 10.5 %copy-start.30 = (f32[16,577]{1,0:T(8,128)}, f32[16,577]{1,0:T(8,128)S(1)}, u32[]{:S(2)}) copy-start(f32[16,577]{1,0:T(8,128)S(1)} %get-tuple-element.139) | copy-start | bytes 110788
  200.1 10.5 %copy-start.18 = (bf16[577,1024]{0,1:T(8,128)(2,1)S(1)}, bf16[577,1024]{0,1:T(8,128)(2,1)}, u32[]{:S(2)}) copy-start(bf16[577,1024]{0,1:T(8,128)(2,1)} %copy.87) | copy-start | bytes 3545092
  210.6 11.7 %copy-start.32 = (f32[16,577]{1,0:T(8,128)}, f32[16,577]{1,0:T(8,128)S(1)}, u32[]{:S(2)}) copy-start(f32[16,577]{1,0:T(8,128)S(1)} %fusion) | copy-start | bytes 110788
  210.7 11.7 %copy-start.16 = (bf16[4,1024,256]{2,1,0:T(8,128)(2,1)S(1)}, bf16[4,1024,256]{2,1,0:T(8,128)(2,1)}, u32[]{:S(2)}) copy-start(bf16[4,1024,256]{2,1,0:T(8,128)(2,1)} %get-tuple-element.110) | copy-start | bytes 6291460
  242.3 7.8 %copy-start.51 = (s32[4]{0:T(128)S(1)}, s32[4]{0:T(128)}, u32[]{:S(2)}) copy-start(s32[4]{0:T(128)} %param.20) | copy-start | bytes 52
  264.0 7.8 %copy-start.8 = (f32[577,1024]{1,0:T(8,128)S(1)}, f32[577,1024]{1,0:T(8,128)}, u32[]{:S(2)}) copy-start(f32[577,1024]{1,0:T(8,128)} %get-tuple-element.142) | copy-start | bytes 7090180
  272.5 11.8 %copy-start.49 = (f32[1024]{0:T(1024)S(1)}, f32[1024]{0:T(1024)}, u32[]{:S(2)}) copy-start(f32[1024]{0:T(1024)} %get-tuple-element.120) | copy-start | bytes 12292
  284.3 12.5 %copy-start.27 = (bf16[577,1024]{1,0:T(8,128)(2,1)S(1)}, bf16[577,1024]{1,0:T(8,128)(2,1)}, u32[]{:S(2)}) copy-start(bf16[577,1024]{1,0:T(8,128)(2,1)} %param.19) | copy-start | bytes 3545092
  296.8 15.1 %copy-start.15 = (bf16[4,1024,1024]{1,2,0:T(8,128)(2,1)S(1)}, bf16[4,1024,1024]{1,2,0:T(8,128)(2,1)}, u32[]{:S(2)}) copy-start(bf16[4,1024,1024]{1,2,0:T(8,128)(2,1)} %pad_maximum_fusion) | copy-start | bytes 25165828
  325.0 11.3 %copy-start.19 = (bf16[577,1024]{0,1:T(8,128)(2,1)S(1)}, bf16[577,1024]{0,1:T(8,128)(2,1)}, u32[]{:S(2)}) copy-start(bf16[577,1024]{0,1:T(8,128)(2,1)} %copy.87) | copy-start | bytes 3545092
  351.4 16.1 %copy-start.2 = (bf16[577,1024]{0,1:T(8,128)(2,1)S(1)}, bf16[577,1024]{0,1:T(8,128)(2,1)}, u32[]{:S(2)}) copy-start(bf16[577,1024]{0,1:T(8,128)(2,1)} %copy-done.1) | copy-start | bytes 3545092
  367.5 4.7 copy-start
  367.5 5.8 copy-start.13
  376.2 8.2 %copy-start.14 = (bf16[4,1024,256]{1,2,0:T(8,128)(2,1)S(1)}, bf16[4,1024,256]{1,2,0:T(8,128)(2,1)}, u32[]{:S(2)}) copy-start(bf16[4,1024,256]{1,2,0:T(8,128)(2,1)} %copy.121) | copy-start | bytes 6291460
  376.2 9.7 %copy-start.26 = (bf16[16,64,577]{2,1,0:T(8,128)(2,1)S(1)}, bf16[16,64,577]{2,1,0:T(8,128)(2,1)}, u32[]{:S(2)}) copy-start(bf16[16,64,577]{2,1,0:T(8,128)(2,1)} %get-tuple-element.150) | copy-start | bytes 3545092
  384.4 7.8 %slice-start = ((s8[9568256]{0:T(1024)(128)(4,1)}), s8[4194304]{0:T(1024)(128)(4,1)S(1)}, s32[]{:S(2)}) async-start(s8[9568256]{0:T(1024)(128)(4,1)} %bitcast.223), calls=%async_computation | async-start | bytes 8388608
  387.5 4.7 slice-start.1
  387.6 4.7 slice-start.2
  409.8 6.0 copy-start.9
  409.8 6.0 copy-start.48
  435.4 5.8 copy-start.52
  456.0 4.0 copy-start.21
  (24 other events, 45.1 us)
